TPU v7x, 256 devices: a whole 4x4x8 slice. The times are simulated.
256 devices in a mesh: step: 4 (over z_hi, core), seq: 64 (over z_lo, y, x).
Axes of the slice: x: 4, y: 4, z: 8 (z_hi: 2, z_lo: 4; z = z_hi * 4 + z_lo), core: 2. Of those that a mesh axis runs over, the one named last changes fastest.
Arguments:
- joined: bfloat16 [8192, 7168], P('seq'), may hold values from -6 to 6
- drafted: bfloat16 [4, 8192, 7168], P('step', 'seq'), may hold values from -6 to 6
- queries: bfloat16 [4, 8192, 3584], P('step', 'seq')
- norm_gain: bfloat16 [7168], replicated, may hold values from 0.099609375 to 1.8984375
- key_matrix: bfloat16 [7168, 512], P('seq', 'step'), may hold values from -0.0625 to 0.0625
- value_matrix: bfloat16 [7168, 512], P('seq', 'step'), may hold values from -0.0625 to 0.0625
Outputs:
- attended: bfloat16 [4, 8192, 3584], P('step', 'seq')
All inputs are finite; a program needn't handle non-finite values.
Results may differ from a plain program's by a relative error of at most 0.006.
The roundings to bfloat16 on the way count: a program that leaves them out, or rounds other values in their place, can miss the bound.
Values may be sent and summed in bfloat16 or wider, within the bound.
A program may use at most 128 MiB of HBM per device.

v0:
```python
import math

import jax
import jax.numpy as jnp
from jax import lax
from jax.sharding import PartitionSpec as P

QH = 28
KVH = 4
HD = 128


def normed(rows, gain):
    values = rows.astype(jnp.float32)
    scaled = values * lax.rsqrt(jnp.mean(values * values, axis=-1, keepdims=True) + 1e-06)
    return (scaled * gain.astype(jnp.float32)).astype(jnp.bfloat16)


def projector(inputs, pieces):
    keys = jnp.einsum("btd,de->bte", inputs, pieces[0], preferred_element_type=jnp.float32)
    values = jnp.einsum("btd,de->bte", inputs, pieces[1], preferred_element_type=jnp.float32)
    return (keys, values)


def per_device(joined, drafted, queries, norm_gain, key_matrix, value_matrix):
    tok = joined.shape[0]
    steps = lax.axis_size("step")
    step_id = lax.axis_index("step")
    seq_id = lax.axis_index("seq")
    group = QH // KVH
    scale = HD ** (-0.5)
    wk_full, wv_full = (
        lax.all_gather(key_matrix, "step", axis=1, tiled=True),
        lax.all_gather(value_matrix, "step", axis=1, tiled=True),
    )
    inputs = normed(jnp.stack([joined, drafted[0]]), norm_gain)
    keys, values = projector(
        inputs,
        (
            lax.all_gather(wk_full, "seq", axis=0, tiled=True),
            lax.all_gather(wv_full, "seq", axis=0, tiled=True),
        ),
    )
    paired = jnp.stack([keys, values], axis=2).astype(jnp.bfloat16)
    context = paired[0]
    diag = lax.all_gather(paired[1:2], "step", axis=0, tiled=True)
    query_rows = queries[0].reshape(tok, KVH, group, HD)
    diag_keys = diag[:, :, 0].reshape(steps, tok, KVH, HD)
    diag_values = diag[:, :, 1].reshape(steps, tok, KVH, HD)
    diag_scores = (
        jnp.einsum("tkgd,jtkd->tkgj", query_rows, diag_keys, preferred_element_type=jnp.float32)
        * scale
    )
    live = jnp.arange(steps) <= step_id
    diag_scores = jnp.where(live[None, None, None, :], diag_scores, -1e30)
    top_start = jnp.max(diag_scores, axis=-1)
    diag_weights = jnp.exp(diag_scores - top_start[..., None])
    total_start = jnp.sum(diag_weights, axis=-1)
    summed_start = jnp.einsum(
        "tkgj,jtkd->tkgd",
        diag_weights.astype(jnp.bfloat16),
        diag_values,
        preferred_element_type=jnp.float32,
    )
    query_offset = seq_id * tok + jnp.arange(tok, dtype=jnp.int32)
    last_query = seq_id * tok + tok - 1
    pieces = (
        lax.all_gather(context[:, 0], "seq", axis=0, tiled=True),
        lax.all_gather(context[:, 1], "seq", axis=0, tiled=True),
    )
    count = pieces[0].shape[0]
    block = math.gcd(count, 1024)

    def one_block(index, state):
        top, total, summed = state
        first = index * block
        block_keys = lax.dynamic_slice_in_dim(pieces[0], first, block, 0).reshape(block, KVH, HD)
        block_values = lax.dynamic_slice_in_dim(pieces[1], first, block, 0).reshape(block, KVH, HD)
        scores = (
            jnp.einsum("tkgd,nkd->tkgn", query_rows, block_keys, preferred_element_type=jnp.float32)
            * scale
        )
        key_pos = first + jnp.arange(block, dtype=jnp.int32)
        allowed = key_pos[None, :] <= query_offset[:, None]
        scores = jnp.where(allowed[:, None, None, :], scores, -1e30)
        new_top = jnp.maximum(top, jnp.max(scores, axis=-1))
        fade = jnp.exp(top - new_top)
        weights = jnp.exp(scores - new_top[..., None])
        total = total * fade + jnp.sum(weights, axis=-1)
        summed = summed * fade[..., None] + jnp.einsum(
            "tkgn,nkd->tkgd",
            weights.astype(jnp.bfloat16),
            block_values,
            preferred_element_type=jnp.float32,
        )
        return (new_top, total, summed)

    reach = jnp.maximum(last_query, -1) // block + 1
    upper = jnp.clip(reach, 0, count // block)
    top, total, summed = lax.fori_loop(
        jnp.int32(0), upper, one_block, (top_start, total_start, summed_start)
    )
    result = summed / total[..., None]
    return result.reshape(1, tok, QH * HD).astype(jnp.bfloat16)


def solution(mesh):
    placed = (
        P("seq", None),
        P("step", "seq", None),
        P("step", "seq", None),
        P(),
        P("seq", "step"),
        P("seq", "step"),
    )
    return jax.shard_map(
        per_device, mesh=mesh, in_specs=placed, out_specs=P("step", "seq", None), check_vma=False
    )
```

profile of v0, /device:TPU:124, one launch (start us, length us, event | category | flops | bytes accessed | tf_op | source)
XLA Modules:
  0.0 1722.3 jit_solution(2288149952912378872)
XLA Ops:
  6.5 10.0 all_gather.21
  16.6 10.1 all_gather.23
  30.3 346.7 %all-gather.8.cloned.1.call-done = bf16[7168,512]{1,0:T(8,128)(2,1)} async-done(((bf16[112,512]{1,0:T(8,128)(2,1)}), bf16[7168,512]{1,0:T(8,128)(2,1)}) %all-gather.8.cloned.1.call-update) | async-done | bytes 7340048 | tf_op jit(solution)/shard_map/all_gather | solution.py:40
  383.3 353.0 %all-gather.10.cloned.1.call-done = bf16[7168,512]{1,0:T(8,128)(2,1)} async-done(((bf16[112,512]{1,0:T(8,128)(2,1)}), bf16[7168,512]{1,0:T(8,128)(2,1)}) %all-gather.10.cloned.1.call-update) | async-done | bytes 7340048 | tf_op jit(solution)/shard_map/all_gather | solution.py:41
  747.2 22.9 %all-gather.12.cloned.1.call-done = bf16[4,128,2,512]{3,1,0,2:T(8,128)(2,1)} async-done(((bf16[1,128,2,512]{3,1,0,2:T(8,128)(2,1)}), bf16[4,128,2,512]{3,1,0,2:T(8,128)(2,1)}) %all-gather.12.cloned.1.call-update) | async-done | bytes 1048592 | tf_op jit(solution)/shard_map/all_gather | solution.py:46
  778.8 353.0 %all-gather.16.cloned.1.call-done = bf16[8192,1,512]{2,0,1:T(8,128)(2,1)} async-done(((bf16[128,1,512]{2,0,1:T(8,128)(2,1)}), bf16[8192,1,512]{2,0,1:T(8,128)(2,1)}) %all-gather.16.cloned.1.call-update) | async-done | bytes 8388624 | tf_op jit(solution)/shard_map/all_gather | solution.py:69
  1131.8 360.7 %all-gather.14.cloned.1.call-done = bf16[8192,1,512]{2,0,1:T(8,128)(2,1)} async-done(((bf16[128,1,512]{2,0,1:T(8,128)(2,1)}), bf16[8192,1,512]{2,0,1:T(8,128)(2,1)}) %all-gather.14.cloned.1.call-update) | async-done | bytes 8388624 | tf_op jit(solution)/shard_map/all_gather | solution.py:68
  1492.5 220.2 %while.15 = (s32[]{:T(128)}, f32[128,4,7]{0,2,1:T(8,128)S(1)}, f32[128,4,7]{0,2,1:T(8,128)S(1)}, f32[128,4,7,128]{0,3,2,1:T(8,128)}, s32[]{:T(128)}, /*index=5*/...) while((s32[]{:T(128)}, f32[128,4,7]{0,2,1:T(8,128)S(1)}, ...), condition=%wide.region_6.7_spmd.clone, body=%wide.region_3.6_spmd.clone.sunk | while | flops 1920475264 | bytes 74556648 | solution.py:100
  1495.5 7.7 fusion.71
  1503.2 8.4 fusion.72
  1511.6 7.2 bitcast_add_fusion.2
  1523.0 7.7 fusion.71
  1530.7 8.4 fusion.72
  1539.1 7.2 bitcast_add_fusion.2
  1550.6 7.7 fusion.71
  1558.2 8.4 fusion.72
  1566.7 7.2 bitcast_add_fusion.2
  1578.1 7.7 fusion.71
  1585.8 8.4 fusion.72
  1594.2 7.2 bitcast_add_fusion.2
  1605.6 7.7 fusion.71
  1613.3 8.4 fusion.72
  1621.7 7.2 bitcast_add_fusion.2
  1633.1 7.7 fusion.71
  1640.8 8.4 fusion.72
  1649.2 7.2 bitcast_add_fusion.2
  1660.7 7.7 fusion.71
  1668.4 8.4 fusion.72
  1676.8 7.2 bitcast_add_fusion.2
  1688.2 7.7 fusion.71
  1695.9 8.4 fusion.72
  1704.3 7.2 bitcast_add_fusion.2
  (140 shorter events, 66.3 us)
Async XLA Ops:
  6.5 370.4 %all-gather.8.cloned.1.call-start = ((), (), s32[]{:S(2)}) async-start(), calls=%async_computation | async-start | bytes 7454720 | tf_op jit(solution)/shard_map/all_gather | solution.py:40
  16.5 719.8 %all-gather.10.cloned.1.call-start = ((), (), s32[]{:S(2)}) async-start(), calls=%async_computation.1 | async-start | bytes 7454720 | tf_op jit(solution)/shard_map/all_gather | solution.py:41
  26.7 743.4 %all-gather.12.cloned.1.call-start = ((), (), s32[]{:S(2)}) async-start(), calls=%async_computation.2 | async-start | bytes 1310720 | tf_op jit(solution)/shard_map/all_gather | solution.py:46
  30.3 706.0 %copy-start.2 = (bf16[1,128,7168]{2,1,0:T(8,128)(2,1)S(1)}, bf16[1,128,7168]{2,1,0:T(8,128)(2,1)}, u32[]{:S(2)}) copy-start(bf16[1,128,7168]{2,1,0:T(8,128)(2,1)} %param.9) | copy-start | bytes 5505028
  383.3 361.0 %copy-start.3 = (bf16[1,128,3584]{2,1,0:T(8,128)(2,1)S(1)}, bf16[1,128,3584]{2,1,0:T(8,128)(2,1)}, u32[]{:S(2)}) copy-start(bf16[1,128,3584]{2,1,0:T(8,128)(2,1)} %param.10) | copy-start | bytes 2752516
  742.9 388.9 %all-gather.16.cloned.1.call-start = ((), (), s32[]{:S(2)}) async-start(), calls=%async_computation.4 | async-start | bytes 8519680 | tf_op jit(solution)/shard_map/all_gather | solution.py:69
  743.7 748.8 %all-gather.14.cloned.1.call-start = ((), (), s32[]{:S(2)}) async-start(), calls=%async_computation.3 | async-start | bytes 8519680 | tf_op jit(solution)/shard_map/all_gather | solution.py:68
  1503.2 8.4 copy-start
  1518.8 1.3 copy-start.1
  1530.7 8.4 copy-start
  1546.3 1.3 copy-start.1
  1558.2 8.4 copy-start
  1573.8 1.3 copy-start.1
  1585.8 8.4 copy-start
  1601.4 1.3 copy-start.1
  1613.3 8.4 copy-start
  1628.9 1.3 copy-start.1
  1640.8 8.4 copy-start
  1656.4 1.3 copy-start.1
  1668.4 8.4 copy-start
  1683.9 1.3 copy-start.1
  1695.9 8.4 copy-start
  1711.5 1.3 copy-start.1
Sparse Core Ops, SparseCore 0:
  16.6 360.2 all-gather.7
  378.8 357.5 all-gather.9
  743.0 27.0 all-gather.11
  771.7 360.0 all-gather.15
  1133.4 359.0 all-gather.13
where the time goes:
time: 1720 us
  waiting for transfers between devices  1440 us (84%)
  matrix products  134 us (8%)
  other arithmetic  75.9 us (4%)
  local copies, waits for them, and re-layouts  41.2 us (2%)
  blocking collectives  20 us (1%)
    all_gather x1, waiting for transfers between devices, per_device(): lax.all_gather(context[:, 0], 'seq', axis=0, tiled=True)  361 us
    all_gather x1, waiting for transfers between devices, per_device(): lax.all_gather(wv_full, 'seq', axis=0, tiled=True)  353 us
    all_gather x1, waiting for transfers between devices, per_device(): lax.all_gather(context[:, 1], 'seq', axis=0, tiled=True)  353 us
    all_gather x1, waiting for transfers between devices, per_device(): lax.all_gather(wk_full, 'seq', axis=0, tiled=True)  347 us
    reduce_sum x8, other arithmetic, one_block(): total = total * fade + jnp.sum(weights, axis=-1)  67 us
    dot_general x8, matrix products, one_block(): jnp.einsum('tkgd,nkd->tkgn', query_rows, block_keys, preferred_element_ty...  61.5 us
    dot_general x8, matrix products, one_block(): jnp.einsum('tkgn,nkd->tkgd', weights.astype(jnp.bfloat16), block_values,...  57.4 us
  transfers between devices with their start and end apart: 5, of which 5 were waited for; matrix products, arithmetic and copies ran while one was open for 1% of the time, Pallas kernels for 0%

commit v1 on v0

v1 whole, which is shorter than its diff:
```python
import functools
import math

import jax
import jax.numpy as jnp
from jax import lax
from jax.experimental import pallas as pl
from jax.experimental.pallas import tpu as pltpu
from jax.sharding import PartitionSpec as P

QH = 28
KVH = 4
HD = 128
GROUP = QH // KVH
D = 7168
TOK = 128
STEPS = 4
ROWS = 112
SIZE = {"x": 4, "y": 4, "z": 8}
ORDER = {"A": "zyx", "B": "zxy", "C": "xyz"}
W_ROWS = {"A": 80, "B": 64, "C": 80}
KV_ROWS = {"A": 48, "B": 48, "C": 32}
MESH = pl.DeviceIdType.MESH
LOG2E = math.log2(math.e)
NEG = -1e30


def position():
    step = lax.axis_index("step")
    seq = lax.axis_index("seq")
    return {
        "z": (step // 2) * 4 + seq // 16,
        "y": lax.rem(seq // 4, 4),
        "x": lax.rem(seq, 4),
        "core": lax.rem(step, 2),
    }


def device(at, **moved):
    at = dict(at)
    for axis, by in moved.items():
        size = SIZE.get(axis, 2)
        at[axis] = lax.rem(at[axis] + by + size, size)
    return (
        (at["z"] // 4) * 2 + at["core"],
        lax.rem(at["z"], 4) * 16 + at["y"] * 4 + at["x"],
    )


def hops(size, split):
    found = []
    for hop in range(1, size // 2):
        found += [(1, hop, None), (-1, hop, None)]
    last = size // 2
    return found + ([(1, last, 0), (-1, last, 1)] if split else [(1, last, None)])


def gather_plan(shard_bytes):
    plan = {}
    for piece, (a1, a2, a3) in ORDER.items():
        n1, n2, n3 = SIZE[a1], SIZE[a2], SIZE[a3]
        unit = shard_bytes[piece]
        first = [(piece, 1, 0, d, k) for d, k, _ in hops(n1, False)]
        for d, k, _ in hops(n1, False):
            plan[piece, 1, 0, d, k] = ((a1, d), unit, [(piece, 1, 0, d, k - 1)] if k > 1 else [])
        for d, k, half in hops(n2, True):
            need = [(piece, 2, 0, d, k - 1)] if k > 1 else first
            plan[piece, 2, 0, d, k] = ((a2, d), unit * n1 // (1 if half is None else 2), need)
        for sub in (0, 1, -1, 2):
            begin = {
                0: first,
                1: [(piece, 2, 0, -1, 1)],
                -1: [(piece, 2, 0, 1, 1)],
                2: [(piece, 2, 0, 1, 2), (piece, 2, 0, -1, 2)],
            }[sub]
            for d, k, half in hops(n3, True):
                need = [(piece, 3, sub, d, k - 1)] if k > 1 else begin
                plan[piece, 3, sub, d, k] = (
                    (a3, d),
                    unit * n1 // (1 if half is None else 2),
                    need,
                )
        for off in range(n3):
            if off == 0:
                need = first + [(piece, 2, 0, d, k) for d, k, _ in hops(n2, True)]
            else:
                need = [
                    (piece, 3, sub, d, k)
                    for sub in (0, 1, -1, 2)
                    for d, k, _ in hops(n3, True)
                    if (-d * k) % n3 == off
                ]
            plan[piece, "core", off] = (("core", 0), unit * n1 * n2, need)
    return plan


def simulate(plan):
    arrive = {}
    free = {}
    waiting = dict(plan)
    while waiting:
        ready = []
        for name, (link, size, need) in waiting.items():
            if all(other in arrive for other in need):
                ready.append((max([arrive[other] for other in need], default=0.0), name))
        ready.sort(key=lambda pair: pair[0])
        at, name = ready[0]
        link, size, _ = waiting.pop(name)
        begin = max(at, free.get(link, 0.0))
        rate = 400e3 if link[0] == "core" else 43e3
        free[link] = begin + size / rate
        arrive[name] = free[link] + 1.0
    return sorted(plan, key=lambda name: arrive[name]), arrive


class Gather:
    def __init__(self, bufs, at, send, recv, base, shard_bytes):
        self.bufs, self.at = bufs, at
        self.send, self.recv, self.base = send, recv, base
        self.plan = gather_plan(shard_bytes)
        self.index = {name: base + i for i, name in enumerate(self.plan)}
        self.order, self.arrive = simulate(self.plan)
        self.got = set()
        self.sent = set()

    def copy(self, name, incoming):
        at = self.at
        buf = self.bufs[name[0]]
        a1, a2, a3 = ORDER[name[0]]
        c = at["core"]
        if name[1] == "core":
            n3 = SIZE[a3]
            q3 = lax.rem(at[a3] + name[2], n3)
            ref = buf.at[1 - c if incoming else c, q3]
            target = device(at, core=1)
        else:
            piece, phase, sub, d, k = name
            axis = ORDER[piece][phase - 1]
            n = SIZE[axis]
            n1 = SIZE[a1]
            back = k if incoming else k - 1
            q = lax.rem(at[axis] - d * back + n, n)
            half = None
            if phase > 1 and k == n // 2:
                half = 0 if d > 0 else 1
            inner = pl.ds(0, n1) if half is None else pl.ds(half * (n1 // 2), n1 // 2)
            if phase == 1:
                ref = buf.at[c, at[a3], at[a2], q]
            elif phase == 2:
                ref = buf.at[c, at[a3], q, inner]
            else:
                q2 = lax.rem(at[a2] + sub + SIZE[a2], SIZE[a2])
                ref = buf.at[c, q, q2, inner]
            target = device(at, **{axis: d})
        i = self.index[name]
        return pltpu.make_async_remote_copy(
            src_ref=ref,
            dst_ref=ref,
            send_sem=self.send.at[i],
            recv_sem=self.recv.at[i],
            device_id=target,
            device_id_type=MESH,
        )

    def start_ready(self):
        for name, (_, _, need) in self.plan.items():
            if name not in self.sent and all(other in self.got for other in need):
                self.sent.add(name)
                self.copy(name, False).start()

    def run(self, tasks=()):
        tasks = list(tasks)
        now = 0.0
        self.start_ready()
        for name in self.order:
            while tasks and now + tasks[0][0] <= self.arrive[name] + 0.3:
                cost, task = tasks.pop(0)
                now += cost
                task()
            now = max(now, self.arrive[name])
            self.copy(name, True).wait_recv()
            self.got.add(name)
            self.start_ready()
        for _, task in tasks:
            task()

    def finish(self):
        for name in self.plan:
            self.copy(name, False).wait_send()


def kernel(
    joined_ref, drafted_ref, queries_ref, gain_ref, key_ref, value_ref, out_ref,
    wa, wb, wc, ka, kb, kc, diag, rows_in, normed, q_held, acc, top, proj, ctx,
    local_sem, w_send, w_recv, k_send, k_recv, d_send, d_recv,
):
    at = position()
    x, y, z, c = at["x"], at["y"], at["z"], at["core"]
    step = lax.axis_index("step")
    z_hi = z // 4
    z_lo = lax.rem(z, 4)

    load_rows = [
        pltpu.make_async_copy(joined_ref, rows_in.at[0], local_sem.at[0]),
        pltpu.make_async_copy(drafted_ref.at[0], rows_in.at[1], local_sem.at[1]),
    ]
    load_q = pltpu.make_async_copy(queries_ref.at[0], q_held, local_sem.at[2])
    for load in load_rows:
        load.start()
    load_q.start()

    wa[c, x, y, z] = key_ref[0:80]
    wb[c, y, x, z, 0:32] = key_ref[80:ROWS]
    wb[c, y, x, z, 32:64] = value_ref[0:32]
    wc[c, z, y, x] = value_ref[32:ROWS]

    barrier = pltpu.get_barrier_semaphore()
    partners = [device(at, x=1), device(at, x=-1), device(at, y=1), device(at, y=-1)]
    partners += [device(at, z=1), device(at, z=-1), device(at, core=1), device(at, z=4)]
    for partner in partners:
        pl.semaphore_signal(barrier, inc=1, device_id=partner, device_id_type=MESH)
    pl.semaphore_wait(barrier, len(partners))

    def norm_rows(which, first, count):
        def body(i, carry):
            start = pl.multiple_of(first + i * 16, 16)
            rows = rows_in[which, pl.ds(start, 16), :].astype(jnp.float32)
            mean = jnp.sum(rows * rows, axis=-1, keepdims=True) * (1.0 / D)
            scaled = rows * lax.rsqrt(mean + 1e-06)
            normed[which, pl.ds(start, 16), :] = (
                scaled * gain_ref[...].astype(jnp.float32)
            ).astype(jnp.bfloat16)
            return carry

        lax.fori_loop(0, count // 16, body, 0)

    def norm_task(which, first):
        def task():
            if first == 0:
                load_rows[which].wait()
            norm_rows(which, first, 32)

        return task

    weights = Gather(
        {"A": wa, "B": wb, "C": wc}, at, w_send, w_recv, 0,
        {piece: rows * HD * 2 for piece, rows in W_ROWS.items()},
    )
    weights.run([(1.0, norm_task(which, 32 * i)) for which in range(2) for i in range(4)])

    proj[...] = jnp.zeros_like(proj)
    ctx[...] = jnp.zeros_like(ctx)

    def project(zz, carry):
        cols = pl.ds(pl.multiple_of(lax.rem(zz, 4) * (16 * ROWS), 128), 16 * ROWS)
        drafted_part = normed[1, :, cols]
        for cc in range(2):
            head = (zz // 4) * 2 + cc
            keys, values = [], []
            for yy in range(4):
                for xx in range(4):
                    keys += [wa[cc, xx, yy, zz], wb[cc, yy, xx, zz, 0:32]]
                    values += [wb[cc, yy, xx, zz, 32:64], wc[cc, zz, yy, xx]]
            both = jnp.concatenate(
                [jnp.concatenate(keys, axis=0), jnp.concatenate(values, axis=0)], axis=1
            )
            proj[head] += jnp.dot(drafted_part, both, preferred_element_type=jnp.float32)

            @pl.when(head == step)
            def _():
                ctx[...] += jnp.dot(
                    normed[0, :, cols], both, preferred_element_type=jnp.float32
                )

        return carry

    lax.fori_loop(0, 8, project, 0)

    held = ctx[...].astype(jnp.bfloat16)
    for kv in range(2):
        part = held[:, kv * HD : (kv + 1) * HD]
        ka[c, x, y, z, kv] = part[0:48]
        kb[c, y, x, z, kv] = part[48:96]
        kc[c, z, y, x, kv] = part[96:128]

    def store_diag(head, carry):
        both = proj[head].astype(jnp.bfloat16)
        for kv in range(2):
            diag[step, head, kv] = both[:, kv * HD : (kv + 1) * HD]
        return carry

    lax.fori_loop(0, KVH, store_diag, 0)

    def diag_copy(which, sem, target):
        return pltpu.make_async_remote_copy(
            src_ref=diag.at[which],
            dst_ref=diag.at[which],
            send_sem=d_send.at[sem],
            recv_sem=d_recv.at[sem],
            device_id=target,
            device_id_type=MESH,
        )

    sibling = device(at, core=1)
    sibling_step = z_hi * 2 + 1 - c
    other = device(at, z=4)
    diag_copy(step, 0, sibling).start()

    @pl.when(z_hi == 0)
    def _():
        diag_copy(step, 1, other).start()

    context = Gather(
        {"A": ka, "B": kb, "C": kc}, at, k_send, k_recv, 0,
        {piece: 2 * rows * HD * 2 for piece, rows in KV_ROWS.items()},
    )
    context.run()
    diag_copy(sibling_step, 0, sibling).wait_recv()

    @pl.when(z_hi == 1)
    def _():
        diag_copy(c, 1, other).wait_recv()
        diag_copy(c, 2, sibling).start()
        diag_copy(1 - c, 2, sibling).wait_recv()
        diag_copy(c, 2, sibling).wait_send()

    diag_copy(step, 0, sibling).wait_send()

    @pl.when(z_hi == 0)
    def _():
        diag_copy(step, 1, other).wait_send()

    load_q.wait()

    acc[...] = jnp.zeros_like(acc)
    top[...] = jnp.full_like(top, NEG)
    scale = LOG2E * HD ** (-0.5)
    row = lax.broadcasted_iota(jnp.int32, (TOK, 1), 0)
    my_seq = lax.axis_index("seq")

    def attend(head, keys, values, bias):
        count = keys.shape[0]
        wide = jnp.concatenate([values, jnp.ones((count, HD), jnp.bfloat16)], axis=1)
        for g in range(GROUP):
            q = q_held[:, pl.ds(pl.multiple_of((head * GROUP + g) * HD, HD), HD)]
            scores = lax.dot_general(
                q, keys, (((1,), (1,)), ((), ())), preferred_element_type=jnp.float32
            ) * scale
            if bias is not None:
                scores = scores + bias
            old = top[head, g]
            new = jnp.maximum(old, jnp.max(scores, axis=-1, keepdims=True))
            top[head, g] = new
            fade = jnp.exp2(old - new)
            p = jnp.exp2(scores - jnp.concatenate([new] * (count // HD), axis=1))
            acc[head, g] = acc[head, g] * jnp.concatenate([fade, fade], axis=1) + jnp.dot(
                p.astype(jnp.bfloat16), wide, preferred_element_type=jnp.float32
            )

    def diag_head(head, carry):
        for pair in range(2):
            keys = diag[pl.ds(2 * pair, 2), head, 0].reshape(2 * TOK, HD)
            values = diag[pl.ds(2 * pair, 2), head, 1].reshape(2 * TOK, HD)
            col = lax.broadcasted_iota(jnp.int32, (TOK, 2 * TOK), 1)
            j = 2 * pair + col // TOK
            ok = jnp.logical_and(lax.rem(col, TOK) == row, j <= step)
            bias = jnp.where(ok, 0.0, NEG)
            ok_rows = j <= step
            attend(head, keys, values, bias)
        return carry

    def key_seq(piece, zz, count, rows):
        col = lax.broadcasted_iota(jnp.int32, (1, count), 1)
        shard = col // rows
        within = lax.rem(col, rows)
        outer, inner = shard // 4, lax.rem(shard, 4)
        if piece == "A":
            xx, yy = outer, inner
        else:
            yy, xx = outer, inner
        start = {"A": 0, "B": 48, "C": 96}[piece]
        return (zz * 16 + yy * 4 + xx) * TOK + start + within

    def plane(zz, masked):
        def body(head, carry):
            zed = (head // 2) * 4 + zz
            core = lax.rem(head, 2)
            for piece, buf in (("A", ka), ("B", kb), ("C", kc)):
                rows = KV_ROWS[piece]
                count = 16 * rows
                if piece == "C":
                    keys = buf[core, zed, :, :, 0].reshape(count, HD)
                    values = buf[core, zed, :, :, 1].reshape(count, HD)
                else:
                    keys = buf[core, :, :, zed, 0].reshape(count, HD)
                    values = buf[core, :, :, zed, 1].reshape(count, HD)
                bias = None
                if masked:
                    ok = key_seq(piece, zz, count, rows) <= my_seq * TOK + row
                    bias = jnp.where(ok, 0.0, NEG)
                attend(head, keys, values, bias)
            return carry

        lax.fori_loop(0, KVH, body, 0)

    lax.fori_loop(0, KVH, diag_head, 0)
    lax.fori_loop(0, z_lo, lambda zz, carry: (plane(zz, False), carry)[1], 0)
    plane(z_lo, True)

    def write(head, carry):
        for g in range(GROUP):
            both = acc[head, g]
            q_held[:, pl.ds(pl.multiple_of((head * GROUP + g) * HD, HD), HD)] = (
                both[:, :HD] / both[:, HD:]
            ).astype(jnp.bfloat16)
        return carry

    lax.fori_loop(0, KVH, write, 0)
    store = pltpu.make_async_copy(q_held, out_ref.at[0], local_sem.at[3])
    store.start()
    weights.finish()
    context.finish()
    store.wait()


def per_device(joined, drafted, queries, norm_gain, key_matrix, value_matrix):
    messages = len(gather_plan({"A": 1, "B": 1, "C": 1}))
    bf16 = jnp.bfloat16
    any_space = pl.BlockSpec(memory_space=pl.ANY)
    vmem = pl.BlockSpec(memory_space=pltpu.VMEM)
    dma = pltpu.SemaphoreType.DMA
    return pl.pallas_call(
        kernel,
        out_shape=jax.ShapeDtypeStruct((1, TOK, QH * HD), bf16),
        in_specs=[any_space, any_space, any_space, vmem, vmem, vmem],
        out_specs=any_space,
        scratch_shapes=[
            pltpu.VMEM((2, 4, 4, 8, 80, HD), bf16),
            pltpu.VMEM((2, 4, 4, 8, 64, HD), bf16),
            pltpu.VMEM((2, 8, 4, 4, 80, HD), bf16),
            pltpu.VMEM((2, 4, 4, 8, 2, 48, HD), bf16),
            pltpu.VMEM((2, 4, 4, 8, 2, 48, HD), bf16),
            pltpu.VMEM((2, 8, 4, 4, 2, 32, HD), bf16),
            pltpu.VMEM((STEPS, KVH, 2, TOK, HD), bf16),
            pltpu.VMEM((2, TOK, D), bf16),
            pltpu.VMEM((2, TOK, D), bf16),
            pltpu.VMEM((TOK, QH * HD), bf16),
            pltpu.VMEM((KVH, GROUP, TOK, 2 * HD), jnp.float32),
            pltpu.VMEM((KVH, GROUP, TOK, HD), jnp.float32),
            pltpu.VMEM((KVH, TOK, 2 * HD), jnp.float32),
            pltpu.VMEM((TOK, 2 * HD), jnp.float32),
            dma((4,)),
            dma((messages,)),
            dma((messages,)),
            dma((messages,)),
            dma((messages,)),
            dma((3,)),
            dma((3,)),
        ],
        compiler_params=pltpu.CompilerParams(
            collective_id=0, has_side_effects=True, vmem_limit_bytes=60 * 2**20
        ),
        cost_estimate=pl.CostEstimate(
            flops=17 * 10**9, bytes_accessed=8 * 10**6, transcendentals=3 * 10**7
        ),
        name="drafter",
    )(joined, drafted, queries, norm_gain.reshape(1, D), key_matrix, value_matrix)


def solution(mesh):
    placed = (
        P("seq", None),
        P("step", "seq", None),
        P("step", "seq", None),
        P(),
        P("seq", "step"),
        P("seq", "step"),
    )
    return jax.shard_map(
        per_device, mesh=mesh, in_specs=placed, out_specs=P("step", "seq", None), check_vma=False
    )
```

time: 1720 us -> 201 us (0.12)
  waiting for transfers between devices: 1440 us -> 0 us
  Pallas kernels: 0 us -> 194 us
  matrix products: 134 us -> 0 us
  other arithmetic: 75.9 us -> 0 us
  local copies, waits for them, and re-layouts: 41.2 us -> 3.5 us
  blocking collectives: 20 us -> 0 us
    all_gather x5 -> x0, waiting for transfers between devices: 1440 us -> none  [the longest x1 361 us: per_device(): lax.all_gather(context[:, 0], 'seq', axis=0, tiled=True)]
    pallas_call x0 -> x1, Pallas kernels: none -> 194 us  [per_device(): pl.pallas_call(kernel, out_shape=jax.ShapeDtypeStruct((1, TOK, QH * HD),...]
    dot_general x20 -> x0, matrix products: 134 us -> none  [the longest x8 61.5 us: one_block(): jnp.einsum('tkgd,nkd->tkgn', query_rows, block_keys, preferred_element_ty...]
    reduce_sum x10 -> x0, other arithmetic: 70.9 us -> none  [the longest x8 67 us: one_block(): total = total * fade + jnp.sum(weights, axis=-1)]
    dynamic_slice x24 -> x0, local copies, waits for them, and re-layouts: 22 us -> none  [the longest x16 17.8 us: one_block(): lax.dynamic_slice_in_dim(pieces[1], first, block, 0).reshape(block, KVH, HD)]
    all_gather x2 -> x0, blocking collectives: 20 us -> none  [the longest x1 10.1 us: per_device(): lax.all_gather(value_matrix, 'step', axis=1, tiled=True)]
  transfers between devices with their start and end apart: 5 -> 0, of which waited for: 5 -> 0; matrix products, arithmetic and copies ran while one was open for 1% -> 0% of each run, Pallas kernels for 0% -> 0%
where the time goes in v1:
time: 201 us; the launch traced here: 197 us
  Pallas kernels  194 us (97%)
  local copies, waits for them, and re-layouts  3.5 us (2%)
    pallas_call x1, Pallas kernels, per_device(): pl.pallas_call(kernel, out_shape=jax.ShapeDtypeStruct((1, TOK, QH * HD),...  194 us

profile of v1, /device:TPU:124, one launch (start us, length us, event | category | flops | bytes accessed | tf_op | source)
XLA Modules:
  0.0 197.3 jit_solution(10504805296675497185)
XLA Ops:
  0.0 1.3 reshape.3.gain_ref
  1.3 193.8 %drafter.1 = bf16[1,128,3584]{2,1,0:T(8,128)(2,1)} custom-call(bf16[128,7168]{1,0:T(8,128)(2,1)} %joined_ref.1, bf16[1,128,7168]{2,1,0:T(8,128)(2,1)} %drafted_ref.1, bf16[1,128,3584]{2,1,0:T(8,128)(2,1)} %queries_ref.1, bf16[1,7168]{1,0:T(2,128)(2,1)} %reshape.3.gain_ref, bf16[112,128]{1,0:T(8,128)(2,1)} %key_ref.1, bf16[112,128]{1,0:T(8,128)(2,1)} %value_ref.1), custom_call_target="tpu_custom_call" | custom-call | flops 16999999488 | bytes 8000000 | tf_op jit(solution)/shard_map/drafter/pallas_call | solution.py:432
  195.2 2.2 %copy.8 = bf16[1,128,3584]{2,1,0:T(8,128)(2,1)} copy(bf16[1,128,3584]{2,1,0:T(8,128)(2,1)} %drafter.1) | data formatting | bytes 1835008
